TPU v7x, 32 devices: a whole 2x2x4 slice. The times are simulated.
32 devices in a mesh: rows: 16 (over z, y, core), img: 2 (over x).
Axes of the slice: x: 2, y: 2, z: 4, core: 2. Of those that a mesh axis runs over, the one named last changes fastest.
Arguments:
- image_in: float32 [16, 256, 88, 128], P('img', 'rows'), may hold values from -30 to 30, as said below
- gain_one: float32 [128], replicated, may hold values from 0.1 to 1.9
- shift_one: float32 [128], replicated, may hold values from -3 to 3
- kernel_one: float32 [3, 3, 128, 128], replicated, may hold values from -0.1875 to 0.1875
- bias_one: float32 [128], replicated, may hold values from -3 to 3
- gain_two: float32 [128], replicated, may hold values from 0.1 to 1.9
- shift_two: float32 [128], replicated, may hold values from -3 to 3
- kernel_two: float32 [3, 3, 128, 128], replicated, may hold values from -0.1875 to 0.1875
- bias_two: float32 [128], replicated, may hold values from -3 to 3
- out_grad: float32 [16, 2, 16, 8, 88, 128], P('rows', 'img'), may hold values from -30 to 30, as said below
Outputs:
- mixed: float32 [16, 2, 16, 8, 88, 128], P('rows', 'img')
- input_grad: float32 [16, 256, 88, 128], P('img', 'rows')
- gain_one_grad: float32 [128], replicated
- shift_one_grad: float32 [128], replicated
- kernel_one_grad: float32 [3, 3, 128, 128], replicated
- bias_one_grad: float32 [128], replicated
- gain_two_grad: float32 [128], replicated
- shift_two_grad: float32 [128], replicated
- kernel_two_grad: float32 [3, 3, 128, 128], replicated
- bias_two_grad: float32 [128], replicated
Inputs may be any that keep to these rules, and one draw needn't show every extreme that they name: `image_in`: feature map of order one with per-channel offsets and scales. `out_grad`: gradient of order one.
All inputs are finite; a program needn't handle non-finite values.
Results may differ from a plain program's by a relative error of at most 0.0003.
Values sent between devices are 32-bit elements; how exact they have to be, the bound alone decides.
No kernel may reach another device: no remote copies, remote signals or barrier semaphores. Data moves between devices by JAX's collectives and lax.ppermute only.
A program may use at most 256 MiB of HBM per device.

v0:
```python
import functools

import jax
import jax.numpy as jnp
from jax import lax
from jax.experimental import pallas as pl
from jax.experimental.pallas import tpu as pltpu
from jax.sharding import PartitionSpec as P

GROUPS = 32
EPSILON = 1e-06
BF16 = jnp.bfloat16
F32 = jnp.float32
MARGIN = 8


def kernel_params():
    return pltpu.CompilerParams(vmem_limit_bytes=48 * 2**20)


def cost(flops, nbytes):
    return pl.CostEstimate(flops=int(flops) // 8, bytes_accessed=int(nbytes) // 8, transcendentals=0)


def split(x):
    high = x.astype(BF16)
    return high, (x - high.astype(F32)).astype(BF16)


def widen(x):
    return jnp.concatenate([x, jnp.zeros((x.shape[0], MARGIN, x.shape[2]), F32)], axis=1)


def put_split(s_ref, row, x):
    channels = x.shape[2]
    high, low = split(widen(x))
    s_ref[row : row + x.shape[0], :, 0:channels] = high
    s_ref[row : row + x.shape[0], :, channels:] = low


def conv_rows(s_ref, w_ref, low_ref, row, rows):
    wide, channels = s_ref.shape[1], s_ref.shape[2] // 2
    m, n = rows * wide, 3 * channels
    high = [s_ref[row + a : row + a + rows, :, 0:channels].reshape(m, channels) for a in range(3)]
    low = [s_ref[row + a : row + a + rows, :, channels:].reshape(m, channels) for a in range(3)]
    y = jnp.dot(jnp.concatenate(high + low[2:], axis=1), w_ref[...], preferred_element_type=F32)
    y = y[:, :n] + y[:, n:]
    y = y + jnp.dot(jnp.concatenate(low[:2], axis=1), low_ref[...], preferred_element_type=F32)
    out = y[:, channels : 2 * channels]
    out = out + pltpu.roll(y[:, :channels], 1, 0) + pltpu.roll(y[:, 2 * channels :], m - 1, 0)
    return out.reshape(rows, wide, channels)[:, : wide - MARGIN]


def row_blocks(total, size):
    return [(r, min(size, total - r)) for r in range(0, total, size)]


def silu(v):
    return v * jax.nn.sigmoid(v)


def silu_slope(v):
    s = jax.nn.sigmoid(v)
    return s * (1.0 + v * (1.0 - s))


def total(x):
    return jnp.sum(x.reshape(-1, x.shape[-1]), axis=0, keepdims=True)


def put_stats(out_ref, i, x):
    count = x.shape[0] * x.shape[1]
    added = total(x)
    mean = added * (1.0 / count)
    off = x - mean[None]
    out_ref[0, pl.ds(i, 1), :] = added
    out_ref[1, pl.ds(i, 1), :] = total(off * off)


def stats_kernel(x_ref, out_ref):
    put_stats(out_ref, pl.program_id(0), x_ref[0])


def conv_one_kernel(edge_ref, x_ref, top_ref, bot_ref, n_ref, w_ref, low_ref, b_ref, mid_ref, act_ref, stat_ref, s_ref):
    i = pl.program_id(0)
    rows = x_ref.shape[1]
    mean, scale, shift = n_ref[0, pl.ds(i, 1)], n_ref[1, pl.ds(i, 1)], n_ref[2, pl.ds(i, 1)]
    act = lambda v: silu((v - mean[None]) * scale[None] + shift[None])
    put_split(s_ref, 0, act(top_ref[0]) * edge_ref[0])
    put_split(s_ref, 2, act(x_ref[0]))
    put_split(s_ref, 2 + rows, act(bot_ref[0]) * edge_ref[1])
    act_ref[0] = s_ref[1 : rows + 3]
    for r, size in row_blocks(rows + 2, 6):
        mid_ref[0, r : r + size] = conv_rows(s_ref, w_ref, low_ref, r, size) + b_ref[...][None]
    put_stats(stat_ref, i, mid_ref[0, 1 : rows + 1])


def conv_two_kernel(edge_ref, mid_ref, x_ref, n_ref, w_ref, low_ref, b_ref, out_ref, act_ref):
    i = pl.program_id(0)
    rows = x_ref.shape[1]
    slab = out_ref.shape[2]
    mean, scale, shift = n_ref[0, pl.ds(i, 1)], n_ref[1, pl.ds(i, 1)], n_ref[2, pl.ds(i, 1)]
    act = lambda v: silu((v - mean[None]) * scale[None] + shift[None])
    s_ref = act_ref.at[0]
    put_split(s_ref, 0, act(mid_ref[0, 0:1]) * edge_ref[0])
    put_split(s_ref, 1, act(mid_ref[0, 1 : rows + 1]))
    put_split(s_ref, 1 + rows, act(mid_ref[0, rows + 1 :]) * edge_ref[1])
    for r, size in row_blocks(rows, slab):
        out_ref[r // slab, 0] = conv_rows(s_ref, w_ref, low_ref, r, size) + b_ref[...][None] + x_ref[0, r : r + size]


def back_two_kernel(band_ref, top_ref, bot_ref, mid_ref, n_ref, w_ref, low_ref, *refs, offsets):
    pieces, (g_ref, out_ref, sum_ref, s_ref) = refs[:-4], refs[-4:]
    i = pl.program_id(0)
    count = len(offsets)
    rows = g_ref.shape[1]
    mean, scale, shift, rstd = (n_ref[k, pl.ds(i, 1)][None] for k in range(4))
    for d in range(len(pieces) // count):
        for s, at in enumerate(offsets):
            piece = pieces[d * count + s]
            _, slab, cols, _ = piece.shape
            g_ref[0, pl.ds(band_ref[d] * slab, slab), at : at + cols, :] = piece[0]
    put_split(s_ref, 0, top_ref[0])
    put_split(s_ref, 1, g_ref[0])
    put_split(s_ref, 1 + rows, bot_ref[0])
    sums = [jnp.zeros((1, g_ref.shape[3]), F32)] * 2
    for r, size in row_blocks(rows, 8):
        off = mid_ref[0, r + 1 : r + 1 + size] - mean
        grad = conv_rows(s_ref, w_ref, low_ref, r, size) * silu_slope(off * scale + shift)
        out_ref[0, r : r + size] = grad
        sums = [sums[0] + total(grad), sums[1] + total(grad * (off * rstd))]
    sum_ref[0, pl.ds(i, 1), :] = sums[0]
    sum_ref[1, pl.ds(i, 1), :] = sums[1]


def taps_kernel(before_ref, act_ref, *refs, offsets, start):
    band_ref, pieces, (out_ref, sum_ref, g_ref, g_scr) = refs[0], refs[1:-4], refs[-4:]
    channels = g_ref.shape[2]
    rows, width, _ = g_ref.shape
    m = rows * width
    i = pl.program_id(0)

    @pl.when(i == 0)
    def _():
        out_ref[...] = before_ref[...]
        g_ref[...] = jnp.zeros_like(g_ref)

    count = len(offsets)
    for k in range(len(pieces) // count):
        for s, at in enumerate(offsets):
            piece = pieces[k * count + s]
            _, slab, cols, _ = piece.shape
            g_ref[pl.ds(band_ref[k] * slab, slab), at : at + cols, :] = piece[0]
    flat = g_ref[...].reshape(m, channels)
    sum_ref[0, pl.ds(i, 1), :] = total(flat)
    column = lax.broadcasted_iota(jnp.int32, (rows, width, channels), 1).reshape(m, channels)
    right = jnp.where(column < width - 1, pltpu.roll(flat, m - 1, 0), 0.0)
    for c, shifted in enumerate((right, flat, pltpu.roll(flat, 1, 0))):
        high, low = split(shifted)
        g_scr[:, c * channels : (c + 1) * channels] = high
        g_scr[:, (c + 3) * channels : (c + 4) * channels] = low
    over_pixels = (((0,), (0,)), ((), ()))
    n = 3 * channels
    for a in range(3):
        high = act_ref[0, a : a + rows, start : start + width, 0:channels].reshape(m, channels)
        low = act_ref[0, a : a + rows, start : start + width, channels:].reshape(m, channels)
        p = lax.dot_general(high, g_scr[...], over_pixels, preferred_element_type=F32)
        q = lax.dot_general(low, g_scr[:, :n], over_pixels, preferred_element_type=F32)
        both = p[:, :n] + p[:, n:] + q
        for c in range(3):
            out_ref[3 * a + c] += both[:, c * channels : (c + 1) * channels]


def back_one_kernel(edge_ref, pre_ref, top_ref, bot_ref, mid_ref, b_ref, g_ref, x_ref, n_ref, w_ref, low_ref, gm_ref, out_ref, sum_ref, s_ref):
    i = pl.program_id(0)
    rows = x_ref.shape[1]
    mid_mean, mid_rstd, gain, first, second = (b_ref[k, pl.ds(i, 1)][None] for k in range(5))
    mean, scale, shift, rstd = (n_ref[k, pl.ds(i, 1)][None] for k in range(4))

    def back(pre, mid):
        normed = (mid - mid_mean) * mid_rstd
        return mid_rstd * (pre * gain - first - normed * second)

    own = back(pre_ref[0], mid_ref[0, 1 : rows + 1])
    gm_ref[0] = own
    put_split(s_ref, 0, back(top_ref[0], mid_ref[0, 0:1]) * edge_ref[0])
    put_split(s_ref, 1, own)
    put_split(s_ref, 1 + rows, back(bot_ref[0], mid_ref[0, rows + 1 :]) * edge_ref[1])
    sum_ref[2, pl.ds(i, 1), :] = total(own)
    sums = [jnp.zeros((1, x_ref.shape[3]), F32)] * 2
    for r, size in row_blocks(rows, 8):
        off = x_ref[0, r : r + size] - mean
        grad = conv_rows(s_ref, w_ref, low_ref, r, size) * silu_slope(off * scale + shift)
        out_ref[0, r : r + size] = g_ref[0, r : r + size] + scale * grad
        sums = [sums[0] + total(grad), sums[1] + total(grad * (off * rstd))]
    sum_ref[0, pl.ds(i, 1), :] = sums[0]
    sum_ref[1, pl.ds(i, 1), :] = sums[1]


def final_kernel(u_ref, x_ref, n_ref, out_ref):
    i = pl.program_id(0)
    mean, rstd, _, first, second = (n_ref[k, pl.ds(i, 1)][None] for k in range(5))
    out_ref[0] = u_ref[0] - rstd * (first + (x_ref[0] - mean) * rstd * second)


def same_group(channels):
    width = channels // GROUPS
    row = lax.broadcasted_iota(jnp.int32, (channels, channels), 0) // width
    col = lax.broadcasted_iota(jnp.int32, (channels, channels), 1) // width
    return (row == col).astype(F32)


def over_group(x):
    return jnp.dot(x, same_group(x.shape[-1]), precision=lax.Precision.HIGHEST, preferred_element_type=F32)


def norm_kernel(all_ref, gain_ref, shift_ref, out_ref, *, local):
    devices, _, _, channels = all_ref.shape
    count = devices * local * (channels // GROUPS)
    added = all_ref[:, 0]
    mean = over_group(jnp.sum(added, axis=0)) * (1.0 / count)
    off = added * (1.0 / local) - mean[None]
    spread = over_group(jnp.sum(all_ref[:, 1] + off * off * float(local), axis=0)) * (1.0 / count)
    rstd = lax.rsqrt(spread + EPSILON)
    out_ref[0] = mean
    out_ref[1] = rstd * gain_ref[...]
    out_ref[2] = jnp.broadcast_to(shift_ref[...], mean.shape)
    out_ref[3] = rstd


def back_norm_kernel(all_ref, n_ref, gain_ref, out_ref, *, local):
    devices, _, _, channels = all_ref.shape
    count = devices * local * (channels // GROUPS)
    out_ref[0] = n_ref[0]
    out_ref[1] = n_ref[3]
    out_ref[2] = jnp.broadcast_to(gain_ref[...], n_ref[0].shape)
    for k in range(2):
        out_ref[3 + k] = over_group(jnp.sum(all_ref[:, k], axis=0) * gain_ref[...]) * (1.0 / count)


def per_image(shape):
    rest = len(shape) - 1
    return pl.BlockSpec((1,) + tuple(shape[1:]), lambda i: (i,) + (0,) * rest)


def whole(shape):
    return pl.BlockSpec(tuple(shape), lambda i: (0,) * len(shape))


SCALARS = pl.BlockSpec(memory_space=pltpu.SMEM)


def call(kernel, images, ins, outs, scratch=(), flops=0):
    nbytes = sum(x.size * x.dtype.itemsize for x, _ in ins)
    shapes = [jax.ShapeDtypeStruct(shape, dtype) for shape, dtype, _ in outs]
    nbytes += sum(s.size * s.dtype.itemsize for s in shapes)
    return pl.pallas_call(
        kernel,
        grid=(images,),
        in_specs=[spec for _, spec in ins],
        out_specs=[spec for _, _, spec in outs],
        out_shape=shapes,
        scratch_shapes=list(scratch),
        compiler_params=kernel_params(),
        cost_estimate=cost(flops, nbytes),
    )(*[x for x, _ in ins])


def img(x):
    return (x, per_image(x.shape))


def all_(x):
    return (x, whole(x.shape))


def small_call(kernel, ins, shape):
    return pl.pallas_call(kernel, out_shape=jax.ShapeDtypeStruct(shape, F32))(*ins)


def weights_kernel(*refs):
    count = len(refs) // 5
    for k in range(count):
        k_ref = refs[k]
        ch = k_ref.shape[2]
        n = 3 * ch
        for turned in (False, True):
            out_ref, low_ref = refs[count + 4 * k + 2 * turned : count + 4 * k + 2 * turned + 2]
            for a in range(3):
                for c in range(3):
                    w = k_ref[2 - a, 2 - c].T if turned else k_ref[a, c]
                    high, low = split(w)
                    out_ref[a * ch : (a + 1) * ch, c * ch : (c + 1) * ch] = high
                    out_ref[a * ch : (a + 1) * ch, n + c * ch : n + (c + 1) * ch] = low
                    if a < 2:
                        low_ref[a * ch : (a + 1) * ch, c * ch : (c + 1) * ch] = high
                    else:
                        out_ref[3 * ch :, c * ch : (c + 1) * ch] = high
            out_ref[3 * ch :, n:] = jnp.zeros((ch, n), BF16)


def prepare(*kernels):
    ch = kernels[0].shape[2]
    shapes = [jax.ShapeDtypeStruct(s, BF16) for s in ((4 * ch, 6 * ch), (2 * ch, 3 * ch))]
    out = pl.pallas_call(
        weights_kernel, out_shape=shapes * (2 * len(kernels)), compiler_params=kernel_params()
    )(*kernels)
    return [out[2 * k : 2 * k + 2] for k in range(2 * len(kernels))]


def after(x, *others):
    return lax.optimization_barrier((x,) + others)[0]


def partner(x, axis, bit):
    return lax.ppermute(x, axis, [(k, k ^ bit) for k in range(lax.axis_size(axis))])


def bits(axis):
    return [1 << k for k in range(lax.axis_size(axis).bit_length() - 1)]


def far_bits():
    low, high = bits("rows")[-2:]
    return low, high, low + high


def gather_sums(x, join):
    for bit in bits("rows")[:-2]:
        x = join(x, partner(x, "rows", bit), bit)
    return jnp.stack([x] + [partner(x, "rows", bit) for bit in far_bits()])


def shift_rows(top_source, bottom_source):
    count = lax.axis_size("rows")
    forward = [(i, i + 1) for i in range(count - 1)]
    backward = [(b, a) for a, b in forward]
    return lax.ppermute(top_source, "rows", forward), lax.ppermute(bottom_source, "rows", backward)


def shift_bands(parts):
    row_devs, count = lax.axis_size("rows"), lax.axis_size("img")
    me = lax.axis_index("img")
    edge = jnp.concatenate([jnp.where(me == 0, p[:, :1], p[:, p.shape[1] - 1 :]) for p in parts], axis=2)
    edge = edge.reshape((count, -1) + edge.shape[1:])
    got = []
    for s in range(count):
        down, up = (count - 1 + s) % count, s
        block = lax.dynamic_index_in_dim(edge, jnp.where(me == 0, up, down), 0, keepdims=False)
        pairs = [(r * count + count - 1, (r + 1) * count + down) for r in range(row_devs - 1)]
        pairs += [(r * count, (r - 1) * count + up) for r in range(1, row_devs)]
        got.append(lax.ppermute(block, ("rows", "img"), pairs))
    got = jnp.stack(got)
    pick = lambda k: lax.dynamic_index_in_dim(got, k, 0, keepdims=False)
    return pick(lax.rem(me + 1, count)), pick(me)


def rotate_img(blocks):
    count = lax.axis_size("img")
    me = lax.axis_index("img")
    pick = lambda k: lax.dynamic_index_in_dim(blocks, lax.rem(k, count), 0, keepdims=False)
    came = [pick(me)]
    for d in range(1, count):
        came.append(lax.ppermute(pick(me + d), "img", [(k, (k + d) % count) for k in range(count)]))
    return came


def img_sources():
    count = lax.axis_size("img")
    me = lax.axis_index("img")
    return [lax.rem(me - d + count, count) for d in range(count)]


def slices(cols, shares):
    units, cuts, seen = cols // 8, [0], 0
    for share in shares[:-1]:
        seen += share
        cuts.append(8 * round(units * seen / sum(shares)))
    cuts.append(cols)
    return [(a, b) for a, b in zip(cuts, cuts[1:]) if b > a]


def swap_rows(x):
    return lax.all_to_all(x, "rows", 0, 0)


def trade(x, axis, bit):
    half = x.shape[0] // 2
    mine = lax.rem(lax.axis_index(axis) // bit, 2)
    keep = lax.dynamic_slice_in_dim(x, mine * half, half, 0)
    give = lax.dynamic_slice_in_dim(x, (1 - mine) * half, half, 0)
    return keep + partner(give, axis, bit)


def untrade(x, axis, bit):
    mine = lax.rem(lax.axis_index(axis) // bit, 2)
    other = partner(x, axis, bit)
    return jnp.where(mine == 0, jnp.concatenate([x, other]), jnp.concatenate([other, x]))


def far_place():
    return lax.axis_index("rows") // far_bits()[0]


def far_trade(x):
    quarter = x.shape[0] // 4
    part = lambda k: lax.dynamic_slice_in_dim(x, k * quarter, quarter, 0)
    place = far_place()
    kept = part(place)
    for d, bit in enumerate(far_bits()):
        kept = kept + partner(part(place ^ (d + 1)), "rows", bit)
    return kept


def far_untrade(x):
    parts = jnp.stack([x] + [partner(x, "rows", bit) for bit in far_bits()])
    place = far_place()
    return jnp.concatenate([lax.dynamic_index_in_dim(parts, place ^ k, 0, keepdims=False) for k in range(4)])


def shards(
    image_in, gain_one, shift_one, kernel_one, bias_one, gain_two, shift_two, kernel_two, bias_two, out_grad
):
    n, rows, cols, ch = image_in.shape
    local = rows * cols
    ext = rows + 2
    wide = cols + MARGIN
    place = lax.axis_index("rows")
    edge = jnp.stack([place > 0, place < lax.axis_size("rows") - 1]).astype(F32)
    edges = (edge, SCALARS)
    row_vec = lambda v: v[None, :]
    conv_flops = 2 * 9 * ch * ch * cols * 3 * n
    pair_shape = (2, n, ch)
    pair = (pair_shape, F32, whole(pair_shape))
    maps = lambda r: ((n, r, cols, ch), F32, per_image((n, r, cols, ch)))
    splits = lambda r: ((n, r, wide, 2 * ch), BF16, per_image((n, r, wide, 2 * ch)))
    taps = ((9, ch, ch), F32, whole((9, ch, ch)))
    row_devs, img_devs = lax.axis_size("rows"), lax.axis_size("img")
    slab = rows // img_devs
    in_cuts = slices(cols, (3, 4, 4))
    out_cuts = slices(cols, (3, 6, 2))
    me = lax.axis_index("img")
    norm = functools.partial(norm_kernel, local=local * row_devs // 4)
    back_norm = functools.partial(back_norm_kernel, local=local * row_devs // 4)
    back_norm_last = functools.partial(back_norm_kernel, local=local * row_devs)
    one_shape = (1, n, ch)
    one = (one_shape, F32, whole(one_shape))

    def join_spread(x, y, bit):
        off = x[0] - y[0]
        return jnp.stack([x[0] + y[0], x[1] + y[1] + off * off * (0.5 / (bit * local))])

    def join_add(x, y, bit):
        return x + y

    grad_in = out_grad.reshape(out_grad.shape[2:])
    landed, came = [], []

    def bring(k, *others):
        a, b = in_cuts[k]
        landed.append(swap_rows(after(grad_in[:, :, a:b], *others)))

    def settle(k, *others):
        a, b = in_cuts[k]
        came.append(rotate_img(after(landed[k], *others).reshape(img_devs, n, slab, b - a, ch)))

    w_one, w_one_back, w_two, w_two_back = prepare(kernel_one, kernel_two)

    top, bottom = shift_rows(image_in[:, rows - 2 :], image_in[:, :2])
    (stat_one,) = call(stats_kernel, n, [img(image_in)], [pair])
    bring(0, stat_one)
    far_one = after(gather_sums(stat_one, join_spread), landed[0], top, bottom)
    n_one = small_call(norm, (far_one, row_vec(gain_one), row_vec(shift_one)), (4, n, ch))
    bring(1, far_one)
    settle(0, far_one)
    middle, act_one, stat_two = call(
        conv_one_kernel,
        n,
        [edges, img(image_in), img(top), img(bottom), all_(n_one), *map(all_, w_one), all_(row_vec(bias_one))],
        [maps(ext), splits(ext), pair],
        [pltpu.VMEM((rows + 4, wide, 2 * ch), BF16)],
        conv_flops * ext,
    )
    far_two = after(gather_sums(after(stat_two, *came[0]), join_spread), landed[1])
    n_two = small_call(norm, (far_two, row_vec(gain_two), row_vec(shift_two)), (4, n, ch))
    bring(2, far_two)
    settle(1, far_two)
    banded_shape = (img_devs, n, slab, cols, ch)
    banded = (banded_shape, F32, pl.BlockSpec((img_devs, 1, slab, cols, ch), lambda i: (0, i, 0, 0, 0)))
    result, act_two = call(
        conv_two_kernel,
        n,
        [edges, img(middle), img(image_in), all_(n_two), *map(all_, w_two), all_(row_vec(bias_two))],
        [banded, splits(ext)],
        (),
        conv_flops * rows,
    )

    def turn(a, b, *others):
        bands = jnp.stack(rotate_img(after(result[..., a:b, :], *others)))
        pick = lambda j: lax.dynamic_index_in_dim(bands, lax.rem(me - j + img_devs, img_devs), 0, keepdims=False)
        return jnp.stack([pick(j) for j in range(img_devs)]).reshape(img_devs * n, slab, b - a, ch)

    mixed_parts = []

    def send(k, *others):
        mixed_parts.append(swap_rows(after(blocks[k], *others)))

    blocks = [turn(*out_cuts[0], *came[1])]
    cut = in_cuts[-1][0]
    offsets = tuple(a for a, _ in in_cuts)
    band = jnp.stack(img_sources()).astype(jnp.int32)

    def add_taps(before, act, parts, at, start, width, bands):
        act_in = img(act)
        if start % width == 0:
            place, start = start // width, 0
            act_in = (act, pl.BlockSpec((1, ext, width, 2 * ch), lambda i: (i, 0, place, 0)))
        return call(
            functools.partial(taps_kernel, offsets=tuple(at), start=start),
            n,
            [all_(before), act_in, (bands, SCALARS)] + [img(p) for line in parts for p in line],
            [taps, one],
            [pltpu.VMEM((rows, width, ch), F32), pltpu.VMEM((rows * width, 6 * ch), BF16)],
            conv_flops * rows * width / wide,
        )

    no_taps = jnp.zeros((9, ch, ch), F32)
    early, late = -(-(cut + 1) // 16) * 16, (cut - 1) // 16 * 16
    by_band = lambda parts: [[part[d] for part in parts] for d in range(img_devs)]
    taps_two, sum_early = add_taps(no_taps, act_two, by_band(came), offsets[:-1], 0, early, band)

    g_top, g_bottom = shift_bands(after(tuple(landed), result))
    settle(2, g_top, g_bottom, blocks[0])
    blocks.append(turn(*out_cuts[1], *came[2]))
    blocks.append(turn(*out_cuts[2], blocks[1]))
    send(0, landed[2], blocks[0], g_top, g_bottom, taps_two)
    grad_result, pre_two, sum_two = call(
        functools.partial(back_two_kernel, offsets=offsets),
        n,
        [(band, SCALARS), img(g_top), img(g_bottom), img(middle), all_(n_two), *map(all_, w_two_back)]
        + [img(p) for line in by_band(came) for p in line],
        [maps(rows), maps(rows), pair],
        [pltpu.VMEM((ext, wide, 2 * ch), BF16)],
        conv_flops * rows,
    )
    pre_top, pre_bottom = shift_rows(pre_two[:, rows - 1 :], pre_two[:, :1])
    far_back = after(gather_sums(sum_two, join_add), mixed_parts[0], blocks[1], pre_top, pre_bottom)
    b_two = small_call(back_norm, (far_back, n_two, row_vec(gain_two)), (5, n, ch))
    send(1, far_back)
    three = ((3, n, ch), F32, whole((3, n, ch)))
    grad_mid, partial, sum_one = call(
        back_one_kernel,
        n,
        [edges, img(pre_two), img(pre_top), img(pre_bottom), img(middle), all_(b_two), img(grad_result), img(image_in), all_(n_one), *map(all_, w_one_back)],
        [maps(rows), maps(rows), three],
        [pltpu.VMEM((ext, wide, 2 * ch), BF16)],
        conv_flops * rows,
    )
    taps_two, sum_late = add_taps(
        taps_two, after(act_two, b_two), by_band(came[-1:]), (cut - late,), late, wide - late, band
    )
    zero = jnp.zeros((1,), jnp.int32)
    taps_one, _ = add_taps(no_taps, after(act_one, blocks[2]), [[grad_mid]], (0,), 0, wide, zero)
    size = 9 * ch
    flat = jnp.concatenate([taps_one.reshape(size, ch), taps_two.reshape(size, ch)])
    steps = [("rows", k) for k in bits("rows")[:-2]] + [("img", k) for k in bits("img")]
    for axis, bit in steps:
        flat = trade(flat, axis, bit)
    sums = jnp.concatenate([sum_one, sum_early + sum_late], axis=0)
    for bit in bits("rows")[:-2]:
        sums = sums + partner(sums, "rows", bit)
    both = after(jnp.concatenate([sums.reshape(-1, ch), flat]), mixed_parts[1])
    both = both + sum(partner(both, "rows", bit) for bit in far_bits())
    far_last, flat = both[: sums.size // ch].reshape((1,) + sums.shape), both[sums.size // ch :]
    b_one = small_call(back_norm_last, (far_last, n_one, row_vec(gain_one)), (5, n, ch))
    empty = jnp.zeros((row_devs, slab, out_cuts[2][1] - out_cuts[2][0], ch), F32)
    mixed = jnp.concatenate(mixed_parts + [empty], axis=2)
    send(2, far_last, flat, mixed)
    (input_grad,) = call(final_kernel, n, [img(partial), img(image_in), all_(b_one)], [maps(rows)])
    for k, (axis, bit) in enumerate(reversed(steps)):
        flat = untrade(flat, axis, bit)
        if k == len(steps) - 1:
            flat = after(flat, input_grad)
    vectors = jnp.concatenate([jnp.sum(far_last, axis=(0, 2)), jnp.sum(far_back, axis=(0, 2))])
    for bit in bits("img"):
        vectors = vectors + partner(vectors, "img", bit)
    last = after(mixed_parts[-1], input_grad, flat, vectors)
    grad_kernel_one, grad_kernel_two = (k.reshape(3, 3, ch, ch) for k in (flat[:size], flat[size:]))
    mixed = lax.dynamic_update_slice_in_dim(mixed, last, out_cuts[2][0], 2)[None, None]
    return (
        mixed,
        input_grad,
        vectors[1],
        vectors[0],
        grad_kernel_one,
        vectors[2],
        vectors[5],
        vectors[4],
        grad_kernel_two,
        vectors[3],
    )


def solution(mesh):
    spread = P("img", "rows", None, None)
    banded = P("rows", "img", None, None, None, None)
    return jax.shard_map(
        shards,
        mesh=mesh,
        in_specs=(spread,) + (P(),) * 8 + (banded,),
        out_specs=(banded, spread) + (P(),) * 8,
        check_vma=False,
    )
```

profile of v0, /device:TPU:9, one launch (start us, length us, event | category | flops | bytes accessed | tf_op | source)
XLA Modules:
  0.0 401.1 jit_solution(1226854651152977618)
XLA Ops:
  9.1 6.6 %all-to-all-start = ((f32[16,8,24,128]{3,2,1,0:T(8,128)}), f32[16,8,24,128]{3,2,1,0:T(8,128)S(1)}, u32[]{:S(2)}, u32[]{:S(2)}) async-start(f32[16,8,24,128]{3,2,1,0:T(8,128)} %slice.164), calls=%async_computation | async-start | bytes 3145728 | tf_op jit(solution)/shard_map/all_to_all | solution.py:384
  27.7 5.0 %fusion.24 = (f32[16,8,32,128]{3,2,1,0:T(8,128)}, f32[16,8,32,128]{3,2,1,0:T(8,128)}) fusion(f32[16,8,88,128]{3,2,1,0:T(8,128)} %bitcast.99), kind=kLoop, calls=%fused_computation.103 | loop fusion | bytes 8388608 | tf_op jit(solution)/shard_map/slice | solution.py:461
  32.7 10.1 %collective-permute-done.4 = f32[2,8,128]{2,1,0:T(8,128)S(1)} collective-permute-done((f32[2,8,128]{2,1,0:T(8,128)S(1)}, f32[2,8,128]{2,1,0:T(8,128)S(1)}, u32[]{:S(2)}, u32[]{:S(2)}) %collective-permute-start.4) | collective-permute-done | bytes 8224 | tf_op jit(solution)/shard_map/ppermute | solution.py:316
  42.8 8.1 %collective-permute-done.5 = f32[2,8,128]{2,1,0:T(8,128)S(1)} collective-permute-done((f32[2,8,128]{2,1,0:T(8,128)S(1)}, f32[2,8,128]{2,1,0:T(8,128)S(1)}, u32[]{:S(2)}, u32[]{:S(2)}) %collective-permute-start.5) | collective-permute-done | bytes 8224 | tf_op jit(solution)/shard_map/ppermute | solution.py:316
  54.6 14.0 %all-to-all-start.1 = ((f32[16,8,32,128]{3,2,1,0:T(8,128)}), f32[16,8,32,128]{3,2,1,0:T(8,128)}, u32[]{:S(2)}, u32[]{:S(2)}) async-start(f32[16,8,32,128]{3,2,1,0:T(8,128)} %get-tuple-element.66), calls=%async_computation.1 | async-start | bytes 4194304 | tf_op jit(solution)/shard_map/all_to_all | solution.py:384
  82.4 21.2 %shard_map.180 = (f32[8,18,88,128]{3,2,1,0:T(8,128)}, bf16[8,18,96,256]{3,2,1,0:T(8,128)(2,1)}, f32[2,8,128]{2,1,0:T(8,128)S(1)}) custom-call(f32[2]{0:T(128)S(1)} %add_convert_fusion.edge_ref, f32[8,16,88,128]{3,2,1,0:T(8,128)} %x_ref.9, f32[8,2,88,128]{3,2,1,0:T(8,128)S(1)} %copy-done.16, f32[8,2,88,128]{3,2,1,0:T(8,128)S(1)} %copy-done.18, ...), custom_call_target="tpu_custom_call" | custom-call | flops 1401421824 | bytes 2722881 | tf_op jit(solution)/shard_map/pallas_call | solution.py:257
  116.7 7.7 %all-to-all-start.2 = ((f32[16,8,32,128]{3,2,1,0:T(8,128)}), f32[16,8,32,128]{3,2,1,0:T(8,128)}, u32[]{:S(2)}, u32[]{:S(2)}) async-start(f32[16,8,32,128]{3,2,1,0:T(8,128)} %get-tuple-element.73), calls=%async_computation.2 | async-start | bytes 4194304 | tf_op jit(solution)/shard_map/all_to_all | solution.py:384
  131.0 17.8 %shard_map.182 = (f32[2,8,8,88,128]{4,3,2,1,0:T(8,128)}, bf16[8,18,96,256]{3,2,1,0:T(8,128)(2,1)}) custom-call(f32[2]{0:T(128)S(1)} %add_convert_fusion.edge_ref, f32[8,18,88,128]{3,2,1,0:T(8,128)} %get-tuple-element.62.mid_ref, f32[8,16,88,128]{3,2,1,0:T(8,128)} %x_ref.9, f32[4,8,128]{2,1,0:T(8,128)S(1)} %copy-done.25, bf16[512,768]{1,0:T(8,128)(2,1)S(1)} %copy-done.14, ...), custom_call_target="tpu_custom_call" | custom-call | flops 1245708288 | bytes 3262529 | tf_op jit(solution)/shard_map/pallas_call | solution.py:257
  153.6 16.9 %all-to-all-done.2 = f32[16,8,32,128]{3,2,1,0:T(8,128)} async-done(((f32[16,8,32,128]{3,2,1,0:T(8,128)}), f32[16,8,32,128]{3,2,1,0:T(8,128)}, u32[]{:S(2)}, u32[]{:S(2)}) %all-to-all-start.2) | async-done | bytes 2097184 | tf_op jit(solution)/shard_map/all_to_all | solution.py:384
  180.7 6.9 %collective-permute-done.15 = f32[8,1,88,128]{3,2,0,1:T(8,128)} collective-permute-done((f32[8,1,88,128]{3,2,0,1:T(8,128)}, f32[8,1,88,128]{3,2,0,1:T(8,128)}, u32[]{:S(2)}, u32[]{:S(2)}) %collective-permute-start.15) | collective-permute-done | bytes 360480 | tf_op jit(solution)/shard_map/ppermute | solution.py:352
  195.9 13.3 %shard_map.183 = (f32[9,128,128]{2,1,0:T(8,128)S(1)}, f32[1,8,128]{2,1,0:T(8,128)S(1)}) custom-call(f32[9,128,128]{2,1,0:T(8,128)S(1)} %broadcast_in_dim.37.before_ref, bf16[8,18,96,256]{3,2,1,0:T(8,128)(2,1)} %get-tuple-element.94.act_ref, s32[2]{0:T(128)S(1)} %pad_add_fusion.refs_0_.band_ref, f32[8,8,24,128]{3,2,1,0:T(8,128)S(1)} %get-tuple-element.125.refs_1_.refs_0_, ...), custom_call_target="tpu_custom_call" | custom-call | flops 830472192 | bytes 1491457 | tf_op jit(solution)/shard_map/pallas_call | solution.py:257
  210.0 5.0 %all-to-all-start.3 = ((f32[16,8,24,128]{3,2,1,0:T(8,128)}), f32[16,8,24,128]{3,2,1,0:T(8,128)}, u32[]{:S(2)}, u32[]{:S(2)}) async-start(f32[16,8,24,128]{3,2,1,0:T(8,128)} %bitcast.97), calls=%async_computation.3 | async-start | bytes 3145728 | tf_op jit(solution)/shard_map/all_to_all | solution.py:384
  220.1 18.4 %shard_map.184 = (f32[8,16,88,128]{3,2,1,0:T(8,128)}, f32[8,16,88,128]{3,2,1,0:T(8,128)}, f32[2,8,128]{2,1,0:T(8,128)S(1)}) custom-call(s32[2]{0:T(128)S(1)} %pad_add_fusion.refs_0_.band_ref, f32[8,1,88,128]{3,2,1,0:T(8,128)S(1)} %copy-done.8, f32[8,1,88,128]{3,2,1,0:T(8,128)S(1)} %copy-done.7, f32[8,18,88,128]{3,2,1,0:T(8,128)} %get-tuple-element.62.mid_ref, ...), custom_call_target="tpu_custom_call" | custom-call | flops 1245708288 | bytes 3189761 | tf_op jit(solution)/shard_map/pallas_call | solution.py:257
  248.2 5.2 %collective-permute-start.24 = (f32[8,1,88,128]{3,2,1,0:T(8,128)S(1)}, f32[8,1,88,128]{3,2,1,0:T(8,128)S(1)}, u32[]{:S(2)}, u32[]{:S(2)}) collective-permute-start(f32[8,1,88,128]{3,2,1,0:T(8,128)S(1)} %get-tuple-element.107), channel_id=1, source_target_pairs={{0,2},{2,4},{4,6},{6,8},{8,10},{10,12},{12,14},{14,16},{16,18},{18... | collective-permute-start | bytes 1081352 | tf_op jit(solution)/shard_map/ppermute | solution.py:338
  258.5 4.3 %collective-permute-done.25.bot_ref = f32[8,1,88,128]{3,2,1,0:T(8,128)S(1)} collective-permute-done((f32[8,1,88,128]{3,2,1,0:T(8,128)S(1)}, f32[8,1,88,128]{3,2,1,0:T(8,128)S(1)}, u32[]{:S(2)}, u32[]{:S(2)}) %collective-permute-start.25) | collective-permute-done | bytes 360480 | tf_op jit(solution)/shard_map/ppermute | solution.py:338
  263.5 4.9 %all-to-all-start.4 = ((f32[16,8,48,128]{3,2,1,0:T(8,128)}), f32[16,8,48,128]{3,2,1,0:T(8,128)}, u32[]{:S(2)}, u32[]{:S(2)}) async-start(f32[16,8,48,128]{3,2,1,0:T(8,128)} %bitcast.95), calls=%async_computation.4 | async-start | bytes 6291456 | tf_op jit(solution)/shard_map/all_to_all | solution.py:384
  272.9 10.4 %shard_map.187 = (f32[9,128,128]{2,1,0:T(8,128)S(1)}, f32[1,8,128]{2,1,0:T(8,128)S(1)}) custom-call(f32[9,128,128]{2,1,0:T(8,128)S(1)} %copy-done.20, bf16[8,18,96,256]{3,2,1,0:T(8,128)(2,1)} %get-tuple-element.94.act_ref, s32[2]{0:T(128)S(1)} %pad_add_fusion.refs_0_.band_ref, f32[8,8,32,128]{3,2,1,0:T(8,128)S(1)} %get-tuple-element.117.refs_2_.refs_1_, ...), custom_call_target="tpu_custom_call" | custom-call | flops 622854144 | bytes 1294849 | tf_op jit(solution)/shard_map/pallas_call | solution.py:257
  283.5 19.9 %shard_map.186 = (f32[8,16,88,128]{3,2,1,0:T(8,128)}, f32[8,16,88,128]{3,2,1,0:T(8,128)}, f32[3,8,128]{2,1,0:T(8,128)S(1)}) custom-call(f32[2]{0:T(128)S(1)} %add_convert_fusion.edge_ref, f32[8,16,88,128]{3,2,1,0:T(8,128)} %get-tuple-element.85.pre_ref, f32[8,1,88,128]{3,2,1,0:T(8,128)S(1)} %collective-permute-done.24.top_ref, ...), custom_call_target="tpu_custom_call" | custom-call | flops 1245708288 | bytes 4634625 | tf_op jit(solution)/shard_map/pallas_call | solution.py:257
  305.7 18.8 %shard_map.188 = (f32[9,128,128]{2,1,0:T(8,128)S(1)}, f32[1,8,128]{2,1,0:T(8,128)}) custom-call(f32[9,128,128]{2,1,0:T(8,128)S(1)} %broadcast_in_dim.37.before_ref, bf16[8,18,96,256]{3,2,1,0:T(8,128)(2,1)} %get-tuple-element.97.act_ref, s32[1]{0:T(128)} %constant.136.clone.1.refs_0_, f32[8,16,88,128]{3,2,1,0:T(8,128)} %get-tuple-element.98.refs_1_), custom_call_target="tpu_custom_call" | custom-call | flops 1245708288 | bytes 1753600 | tf_op jit(solution)/shard_map/pallas_call | solution.py:257
  330.6 9.8 %collective-permute-done.30 = f32[576,128]{1,0:T(8,128)S(1)} collective-permute-done((f32[576,128]{1,0:T(8,128)S(1)}, f32[576,128]{1,0:T(8,128)S(1)}, u32[]{:S(2)}, u32[]{:S(2)}) %collective-permute-start.30) | collective-permute-done | bytes 294944 | tf_op jit(solution)/shard_map/ppermute | solution.py:316
  351.7 10.0 %collective-permute-done.34 = f32[320,128]{1,0:T(8,128)S(1)} collective-permute-done((f32[320,128]{1,0:T(8,128)S(1)}, f32[320,128]{1,0:T(8,128)S(1)}, u32[]{:S(2)}, u32[]{:S(2)}) %collective-permute-start.34) | collective-permute-done | bytes 163872 | tf_op jit(solution)/shard_map/ppermute | solution.py:316
  367.5 7.6 %all-to-all-start.5 = ((f32[16,8,16,128]{3,2,1,0:T(8,128)}), f32[16,8,16,128]{3,2,1,0:T(8,128)S(1)}, u32[]{:S(2)}, u32[]{:S(2)}) async-start(f32[16,8,16,128]{3,2,1,0:T(8,128)} %bitcast.48), calls=%async_computation.5 | async-start | bytes 2097152 | tf_op jit(solution)/shard_map/all_to_all | solution.py:384
  375.6 5.6 %fusion.22 = f32[1,1,16,8,88,128]{5,4,3,2,1,0:T(8,128)} fusion(f32[88]{0:T(128)S(1)} %pad.26.clone, f32[16,8,48,128]{3,2,1,0:T(8,128)} %all-to-all-done.4, f32[16,8,24,128]{3,2,1,0:T(8,128)} %all-to-all-done.3), kind=kLoop, calls=%fused_computation.101 | loop fusion | flops 2883584 | bytes 10486112 | tf_op jit(solution)/shard_map/broadcast_in_dim | solution.py:590
  386.1 8.0 %shard_map.190 = f32[8,16,88,128]{3,2,1,0:T(8,128)} custom-call(f32[8,16,88,128]{3,2,1,0:T(8,128)S(1)} %copy-done.1, f32[8,16,88,128]{3,2,1,0:T(8,128)} %x_ref.9, f32[5,8,128]{2,1,0:T(8,128)S(1)} %copy-done.37), custom_call_target="tpu_custom_call" | custom-call | bytes 2165248 | tf_op jit(solution)/shard_map/pallas_call | solution.py:257
  (237 shorter events, 144.4 us)
Async XLA Ops:
  9.1 45.5 %all-to-all-start = ((f32[16,8,24,128]{3,2,1,0:T(8,128)}), f32[16,8,24,128]{3,2,1,0:T(8,128)S(1)}, u32[]{:S(2)}, u32[]{:S(2)}) async-start(f32[16,8,24,128]{3,2,1,0:T(8,128)} %slice.164), calls=%async_computation | async-start | bytes 3145728 | tf_op jit(solution)/shard_map/all_to_all | solution.py:384
  19.6 33.2 %collective-permute-start = (f32[8,2,88,128]{3,2,1,0:T(8,128)S(1)}, f32[8,2,88,128]{3,2,1,0:T(8,128)S(1)}, u32[]{:S(2)}, u32[]{:S(2)}) collective-permute-start(f32[8,2,88,128]{3,2,1,0:T(8,128)S(1)} %get-tuple-element.111), channel_id=1, source_target_pairs={{0,2},{2,4},{4,6},{6,8},{8,10},{10,12},{12,14},{14,16},{16,18},{18... | collective-permute-start | bytes 2162696 | tf_op jit(solution)/shard_map/ppermute | solution.py:338
  22.3 31.3 %collective-permute-start.1 = (f32[8,2,88,128]{3,2,1,0:T(8,128)S(1)}, f32[8,2,88,128]{3,2,1,0:T(8,128)S(1)}, u32[]{:S(2)}, u32[]{:S(2)}) collective-permute-start(f32[8,2,88,128]{3,2,1,0:T(8,128)S(1)} %get-tuple-element.110), channel_id=1, source_target_pairs={{2,0},{4,2},{6,4},{8,6},{10,8},{12,10},{14,12},{16,14},{18,16},{20... | collective-permute-start | bytes 2162696 | tf_op jit(solution)/shard_map/ppermute | solution.py:338
  24.3 18.5 %collective-permute-start.4 = (f32[2,8,128]{2,1,0:T(8,128)S(1)}, f32[2,8,128]{2,1,0:T(8,128)S(1)}, u32[]{:S(2)}, u32[]{:S(2)}) collective-permute-start(f32[2,8,128]{2,1,0:T(8,128)S(1)} %get-tuple-element.147), channel_id=1, source_target_pairs={{0,8},{2,10},{4,12},{6,14},{8,0},{10,2},{12,4},{14,6},{16,24},{18,... | collective-permute-start | bytes 24584 | tf_op jit(solution)/shard_map/ppermute | solution.py:316
  25.8 25.1 %collective-permute-start.5 = (f32[2,8,128]{2,1,0:T(8,128)S(1)}, f32[2,8,128]{2,1,0:T(8,128)S(1)}, u32[]{:S(2)}, u32[]{:S(2)}) collective-permute-start(f32[2,8,128]{2,1,0:T(8,128)S(1)} %get-tuple-element.147), channel_id=1, source_target_pairs={{0,16},{2,18},{4,20},{6,22},{8,24},{10,26},{12,28},{14,30},{16,0},... | collective-permute-start | bytes 24584 | tf_op jit(solution)/shard_map/ppermute | solution.py:316
  27.5 24.6 %collective-permute-start.6 = (f32[2,8,128]{2,1,0:T(8,128)S(1)}, f32[2,8,128]{2,1,0:T(8,128)S(1)}, u32[]{:S(2)}, u32[]{:S(2)}) collective-permute-start(f32[2,8,128]{2,1,0:T(8,128)S(1)} %get-tuple-element.147), channel_id=1, source_target_pairs={{0,24},{2,26},{4,28},{6,30},{8,16},{10,18},{12,20},{14,22},{16,8},... | collective-permute-start | bytes 24584 | tf_op jit(solution)/shard_map/ppermute | solution.py:316
  54.6 62.1 %all-to-all-start.1 = ((f32[16,8,32,128]{3,2,1,0:T(8,128)}), f32[16,8,32,128]{3,2,1,0:T(8,128)}, u32[]{:S(2)}, u32[]{:S(2)}) async-start(f32[16,8,32,128]{3,2,1,0:T(8,128)} %get-tuple-element.66), calls=%async_computation.1 | async-start | bytes 4194304 | tf_op jit(solution)/shard_map/all_to_all | solution.py:384
  69.6 34.0 %collective-permute-start.7 = (f32[8,8,24,128]{3,2,1,0:T(8,128)}, f32[8,8,24,128]{3,2,1,0:T(8,128)S(1)}, u32[]{:S(2)}, u32[]{:S(2)}) collective-permute-start(f32[8,8,24,128]{3,2,1,0:T(8,128)} %get-tuple-element.124), channel_id=1, source_target_pairs={{0,1},{1,0},{2,3},{3,2},{4,5},{5,4},{6,7},{7,6},{8,9},{9,8},{10,11... | collective-permute-start | bytes 2359304 | tf_op jit(solution)/shard_map/ppermute | solution.py:364
  116.7 53.8 %all-to-all-start.2 = ((f32[16,8,32,128]{3,2,1,0:T(8,128)}), f32[16,8,32,128]{3,2,1,0:T(8,128)}, u32[]{:S(2)}, u32[]{:S(2)}) async-start(f32[16,8,32,128]{3,2,1,0:T(8,128)} %get-tuple-element.73), calls=%async_computation.2 | async-start | bytes 4194304 | tf_op jit(solution)/shard_map/all_to_all | solution.py:384
  127.3 24.7 %collective-permute-start.13 = (f32[8,8,32,128]{3,2,1,0:T(8,128)}, f32[8,8,32,128]{3,2,1,0:T(8,128)S(1)}, u32[]{:S(2)}, u32[]{:S(2)}) collective-permute-start(f32[8,8,32,128]{3,2,1,0:T(8,128)} %get-tuple-element.118), channel_id=1, source_target_pairs={{0,1},{1,0},{2,3},{3,2},{4,5},{5,4},{6,7},{7,6},{8,9},{9,8},{10,11... | collective-permute-start | bytes 3145736 | tf_op jit(solution)/shard_map/ppermute | solution.py:364
  153.6 24.4 %collective-permute-start.14 = (f32[8,8,24,128]{3,2,1,0:T(8,128)}, f32[8,8,24,128]{3,2,1,0:T(8,128)}, u32[]{:S(2)}, u32[]{:S(2)}) collective-permute-start(f32[8,8,24,128]{3,2,1,0:T(8,128)} %get-tuple-element.122), channel_id=1, source_target_pairs={{0,1},{1,0},{2,3},{3,2},{4,5},{5,4},{6,7},{7,6},{8,9},{9,8},{10,11... | collective-permute-start | bytes 2359304 | tf_op jit(solution)/shard_map/ppermute | solution.py:364
  173.7 13.9 %collective-permute-start.15 = (f32[8,1,88,128]{3,2,0,1:T(8,128)}, f32[8,1,88,128]{3,2,0,1:T(8,128)}, u32[]{:S(2)}, u32[]{:S(2)}) collective-permute-start(f32[8,1,88,128]{3,2,0,1:T(8,128)} %get-tuple-element.135), channel_id=1, source_target_pairs={{1,3},{3,5},{5,7},{7,9},{9,11},{11,13},{13,15},{15,17},{17,19},{19... | collective-permute-start | bytes 1081352 | tf_op jit(solution)/shard_map/ppermute | solution.py:352
  175.8 11.9 %collective-permute-start.16 = (f32[8,1,88,128]{3,2,0,1:T(8,128)S(1)}, f32[8,1,88,128]{3,2,0,1:T(8,128)}, u32[]{:S(2)}, u32[]{:S(2)}) collective-permute-start(f32[8,1,88,128]{3,2,0,1:T(8,128)S(1)} %get-tuple-element.134), channel_id=1, source_target_pairs={{1,2},{3,4},{5,6},{7,8},{9,10},{11,12},{13,14},{15,16},{17,18},{19... | collective-permute-start | bytes 1081352 | tf_op jit(solution)/shard_map/ppermute | solution.py:352
  192.6 25.8 %collective-permute-start.17 = (f32[8,8,32,128]{3,2,1,0:T(8,128)}, f32[8,8,32,128]{3,2,1,0:T(8,128)}, u32[]{:S(2)}, u32[]{:S(2)}) collective-permute-start(f32[8,8,32,128]{3,2,1,0:T(8,128)} %get-tuple-element.116), channel_id=1, source_target_pairs={{0,1},{1,0},{2,3},{3,2},{4,5},{5,4},{6,7},{7,6},{8,9},{9,8},{10,11... | collective-permute-start | bytes 3145736 | tf_op jit(solution)/shard_map/ppermute | solution.py:364
  210.0 52.7 %all-to-all-start.3 = ((f32[16,8,24,128]{3,2,1,0:T(8,128)}), f32[16,8,24,128]{3,2,1,0:T(8,128)}, u32[]{:S(2)}, u32[]{:S(2)}) async-start(f32[16,8,24,128]{3,2,1,0:T(8,128)} %bitcast.97), calls=%async_computation.3 | async-start | bytes 3145728 | tf_op jit(solution)/shard_map/all_to_all | solution.py:384
  218.8 37.2 %collective-permute-start.18 = (f32[8,8,48,128]{3,2,1,0:T(8,128)S(1)}, f32[8,8,48,128]{3,2,1,0:T(8,128)S(1)}, u32[]{:S(2)}, u32[]{:S(2)}) collective-permute-start(f32[8,8,48,128]{3,2,1,0:T(8,128)S(1)} %get-tuple-element.114), channel_id=1, source_target_pairs={{0,1},{1,0},{2,3},{3,2},{4,5},{5,4},{6,7},{7,6},{8,9},{9,8},{10,11... | collective-permute-start | bytes 4718600 | tf_op jit(solution)/shard_map/ppermute | solution.py:364
  263.5 81.5 %all-to-all-start.4 = ((f32[16,8,48,128]{3,2,1,0:T(8,128)}), f32[16,8,48,128]{3,2,1,0:T(8,128)}, u32[]{:S(2)}, u32[]{:S(2)}) async-start(f32[16,8,48,128]{3,2,1,0:T(8,128)} %bitcast.95), calls=%async_computation.4 | async-start | bytes 6291456 | tf_op jit(solution)/shard_map/all_to_all | solution.py:384
  270.7 32.6 %collective-permute-start.26 = (f32[8,8,16,128]{3,2,1,0:T(8,128)}, f32[8,8,16,128]{3,2,1,0:T(8,128)}, u32[]{:S(2)}, u32[]{:S(2)}) collective-permute-start(f32[8,8,16,128]{3,2,1,0:T(8,128)} %get-tuple-element.130), channel_id=1, source_target_pairs={{0,1},{1,0},{2,3},{3,2},{4,5},{5,4},{6,7},{7,6},{8,9},{9,8},{10,11... | collective-permute-start | bytes 1572872 | tf_op jit(solution)/shard_map/ppermute | solution.py:364
  327.6 12.8 %collective-permute-start.30 = (f32[576,128]{1,0:T(8,128)S(1)}, f32[576,128]{1,0:T(8,128)S(1)}, u32[]{:S(2)}, u32[]{:S(2)}) collective-permute-start(f32[576,128]{1,0:T(8,128)S(1)} %constant_dynamic-slice_fusion.1), channel_id=1, source_target_pairs={{0,4},{2,6},{4,0},{6,2},{8,12},{10,14},{12,8},{14,10},{16,20},{18,... | collective-permute-start | bytes 884744 | tf_op jit(solution)/shard_map/ppermute | solution.py:316
  330.3 11.1 %collective-permute-start.28 = (f32[4,8,128]{2,1,0:T(8,128)S(1)}, f32[4,8,128]{2,1,0:T(8,128)S(1)}, u32[]{:S(2)}, u32[]{:S(2)}) collective-permute-start(f32[4,8,128]{2,1,0:T(8,128)S(1)} %fusion.21), channel_id=1, source_target_pairs={{0,4},{2,6},{4,0},{6,2},{8,12},{10,14},{12,8},{14,10},{16,20},{18,... | collective-permute-start | bytes 49160 | tf_op jit(solution)/shard_map/ppermute | solution.py:316
  346.7 15.0 %collective-permute-start.34 = (f32[320,128]{1,0:T(8,128)S(1)}, f32[320,128]{1,0:T(8,128)S(1)}, u32[]{:S(2)}, u32[]{:S(2)}) collective-permute-start(f32[320,128]{1,0:T(8,128)S(1)} %pad_maximum_fusion.4), channel_id=1, source_target_pairs={{0,24},{2,26},{4,28},{6,30},{8,16},{10,18},{12,20},{14,22},{16,8},... | collective-permute-start | bytes 491528 | tf_op jit(solution)/shard_map/ppermute | solution.py:316
  366.0 28.1 %collective-permute-start.38 = (f32[6,128]{1,0:T(8,128)S(1)}, f32[6,128]{1,0:T(8,128)S(1)}, u32[]{:S(2)}, u32[]{:S(2)}) collective-permute-start(f32[6,128]{1,0:T(8,128)S(1)} %pad_maximum_fusion.13), channel_id=1, source_target_pairs={{0,1},{1,0},{2,3},{3,2},{4,5},{5,4},{6,7},{7,6},{8,9},{9,8},{10,11... | collective-permute-start | bytes 9224 | tf_op jit(solution)/shard_map/ppermute | solution.py:316
  367.5 32.5 %all-to-all-start.5 = ((f32[16,8,16,128]{3,2,1,0:T(8,128)}), f32[16,8,16,128]{3,2,1,0:T(8,128)S(1)}, u32[]{:S(2)}, u32[]{:S(2)}) async-start(f32[16,8,16,128]{3,2,1,0:T(8,128)} %bitcast.48), calls=%async_computation.5 | async-start | bytes 2097152 | tf_op jit(solution)/shard_map/all_to_all | solution.py:384
  375.2 19.4 %collective-permute-start.37 = (f32[1152,128]{1,0:T(8,128)S(1)}, f32[1152,128]{1,0:T(8,128)S(1)}, u32[]{:S(2)}, u32[]{:S(2)}) collective-permute-start(f32[1152,128]{1,0:T(8,128)S(1)} %maximum_select_fusion.1), channel_id=1, source_target_pairs={{0,2},{2,0},{4,6},{6,4},{8,10},{10,8},{12,14},{14,12},{16,18},{18,... | collective-permute-start | bytes 1769480 | tf_op jit(solution)/shard_map/ppermute | solution.py:316
  (66 other events, 371.1 us)
where the time goes:
time: 403 us; the launch traced here: 401 us
  Pallas kernels  138 us (34%)
  waiting for transfers between devices  98.3 us (24%)
  starting transfers between devices  92.4 us (23%)
  local copies, waits for them, and re-layouts  50.2 us (12%)
  other arithmetic  20.7 us (5%)
    pallas_call x9, Pallas kernels, call(): pl.pallas_call(kernel, grid=(images,), in_specs=[spec for _, spec in ins]...  131 us
    ppermute x27, waiting for transfers between devices, partner(): lax.ppermute(x, axis, [(k, k ^ bit) for k in range(lax.axis_size(axis))])  63.1 us
    all_to_all x6, starting transfers between devices, swap_rows(): return lax.all_to_all(x, 'rows', 0, 0)  45.8 us
    ppermute x27, starting transfers between devices, partner(): lax.ppermute(x, axis, [(k, k ^ bit) for k in range(lax.axis_size(axis))])  25 us
    all_to_all x6, waiting for transfers between devices, swap_rows(): return lax.all_to_all(x, 'rows', 0, 0)  21.1 us
    unnamed x90, local copies, waits for them, and re-layouts  21 us
    squeeze x6, local copies, waits for them, and re-layouts, rotate_img(): lax.dynamic_index_in_dim(blocks, lax.rem(k, count), 0, keepdims=False)  9.56 us
  transfers between devices with their start and end apart: 45, of which 24 were waited for; matrix products, arithmetic and copies ran while one was open for 10% of the time, Pallas kernels for 34%

commit v1 on v0

--- a/solution.py
+++ b/solution.py
@@ -570,9 +570,15 @@
     sums = jnp.concatenate([sum_one, sum_early + sum_late], axis=0)
     for bit in bits("rows")[:-2]:
         sums = sums + partner(sums, "rows", bit)
-    both = after(jnp.concatenate([sums.reshape(-1, ch), flat]), mixed_parts[1])
-    both = both + sum(partner(both, "rows", bit) for bit in far_bits())
-    far_last, flat = both[: sums.size // ch].reshape((1,) + sums.shape), both[sums.size // ch :]
+    sums_in, flat = after((sums.reshape(-1, ch), flat), mixed_parts[1])
+    quarter = flat.shape[0] // 4
+    place = lax.axis_index("rows") // far_bits()[0]
+    with_sums = lambda k: jnp.concatenate([sums_in, lax.dynamic_slice_in_dim(flat, k * quarter, quarter, 0)])
+    both = with_sums(place)
+    both = both + sum(partner(with_sums(place ^ (d + 1)), "rows", bit) for d, bit in enumerate(far_bits()))
+    far_last, flat = both[: sums_in.shape[0]].reshape((1,) + sums.shape), both[sums_in.shape[0] :]
+    flat = jnp.stack([flat] + [partner(flat, "rows", bit) for bit in far_bits()])
+    flat = jnp.concatenate([lax.dynamic_index_in_dim(flat, place ^ k, 0, keepdims=False) for k in range(4)])
     b_one = small_call(back_norm_last, (far_last, n_one, row_vec(gain_one)), (5, n, ch))
     empty = jnp.zeros((row_devs, slab, out_cuts[2][1] - out_cuts[2][0], ch), F32)
     mixed = jnp.concatenate(mixed_parts + [empty], axis=2)

time: 403 us -> 406 us (level)
  starting transfers between devices: 92.4 us -> 110 us
  waiting for transfers between devices: 98.3 us -> 82.4 us
    ppermute x27 -> x30, waiting for transfers between devices: 63.1 us -> 51 us  [partner(): lax.ppermute(x, axis, [(k, k ^ bit) for k in range(lax.axis_size(axis))])]
    all_to_all x6, starting transfers between devices: 45.8 us -> 53.5 us  [swap_rows(): return lax.all_to_all(x, 'rows', 0, 0)]
    ppermute x27 -> x30, starting transfers between devices: 25 us -> 30.3 us  [partner(): lax.ppermute(x, axis, [(k, k ^ bit) for k in range(lax.axis_size(axis))])]
    unnamed x90 -> x98, local copies, waits for them, and re-layouts: 21 us -> 21.7 us
  transfers between devices with their start and end apart: 45 -> 48, of which waited for: 24 -> 29; matrix products, arithmetic and copies ran while one was open for 10% -> 11% of each run, Pallas kernels for 34% -> 33%
where the time goes in v1:
time: 406 us; the launch traced here: 404 us
  Pallas kernels  137 us (34%)
  starting transfers between devices  110 us (27%)
  waiting for transfers between devices  82.4 us (20%)
  local copies, waits for them, and re-layouts  52.3 us (13%)
  other arithmetic  20.7 us (5%)
    pallas_call x9, Pallas kernels, call(): pl.pallas_call(kernel, grid=(images,), in_specs=[spec for _, spec in ins]...  130 us
    all_to_all x6, starting transfers between devices, swap_rows(): return lax.all_to_all(x, 'rows', 0, 0)  53.5 us
    ppermute x30, waiting for transfers between devices, partner(): lax.ppermute(x, axis, [(k, k ^ bit) for k in range(lax.axis_size(axis))])  51 us
    ppermute x30, starting transfers between devices, partner(): lax.ppermute(x, axis, [(k, k ^ bit) for k in range(lax.axis_size(axis))])  30.3 us
    unnamed x98, local copies, waits for them, and re-layouts  21.7 us
    all_to_all x6, waiting for transfers between devices, swap_rows(): return lax.all_to_all(x, 'rows', 0, 0)  20.1 us
    squeeze x6, local copies, waits for them, and re-layouts, rotate_img(): lax.dynamic_index_in_dim(blocks, lax.rem(k, count), 0, keepdims=False)  10.9 us
  transfers between devices with their start and end apart: 48, of which 29 were waited for; matrix products, arithmetic and copies ran while one was open for 11% of the time, Pallas kernels for 33%

profile of v1, /device:TPU:9, one launch (start us, length us, event | category | flops | bytes accessed | tf_op | source)
XLA Modules:
  0.0 403.9 jit_solution(11934265659681094471)
XLA Ops:
  9.1 6.6 %all-to-all-start = ((f32[16,8,24,128]{3,2,1,0:T(8,128)}), f32[16,8,24,128]{3,2,1,0:T(8,128)S(1)}, u32[]{:S(2)}, u32[]{:S(2)}) async-start(f32[16,8,24,128]{3,2,1,0:T(8,128)} %slice.164), calls=%async_computation | async-start | bytes 3145728 | tf_op jit(solution)/shard_map/all_to_all | solution.py:384
  27.9 5.0 %fusion.25 = (f32[16,8,32,128]{3,2,1,0:T(8,128)}, f32[16,8,32,128]{3,2,1,0:T(8,128)}) fusion(f32[16,8,88,128]{3,2,1,0:T(8,128)} %bitcast.116), kind=kLoop, calls=%fused_computation.127 | loop fusion | bytes 8388608 | tf_op jit(solution)/shard_map/slice | solution.py:461
  32.9 18.0 %collective-permute-done.5 = f32[2,8,128]{2,1,0:T(8,128)S(1)} collective-permute-done((f32[2,8,128]{2,1,0:T(8,128)S(1)}, f32[2,8,128]{2,1,0:T(8,128)S(1)}, u32[]{:S(2)}, u32[]{:S(2)}) %collective-permute-start.5) | collective-permute-done | bytes 8224 | tf_op jit(solution)/shard_map/ppermute | solution.py:316
  55.8 14.0 %all-to-all-start.1 = ((f32[16,8,32,128]{3,2,1,0:T(8,128)}), f32[16,8,32,128]{3,2,1,0:T(8,128)}, u32[]{:S(2)}, u32[]{:S(2)}) async-start(f32[16,8,32,128]{3,2,1,0:T(8,128)} %get-tuple-element.67), calls=%async_computation.1 | async-start | bytes 4194304 | tf_op jit(solution)/shard_map/all_to_all | solution.py:384
  85.1 21.1 %shard_map.180 = (f32[8,18,88,128]{3,2,1,0:T(8,128)}, bf16[8,18,96,256]{3,2,1,0:T(8,128)(2,1)}, f32[2,8,128]{2,1,0:T(8,128)S(1)}) custom-call(f32[2]{0:T(128)S(1)} %add_convert_fusion.edge_ref, f32[8,16,88,128]{3,2,1,0:T(8,128)} %x_ref.9, f32[8,2,88,128]{3,2,1,0:T(8,128)S(1)} %copy-done.18, f32[8,2,88,128]{3,2,1,0:T(8,128)S(1)} %copy-done.16, ...), custom_call_target="tpu_custom_call" | custom-call | flops 1401421824 | bytes 2722881 | tf_op jit(solution)/shard_map/pallas_call | solution.py:257
  110.3 3.5 collective-permute-start.11
  117.8 8.6 %all-to-all-start.2 = ((f32[16,8,32,128]{3,2,1,0:T(8,128)}), f32[16,8,32,128]{3,2,1,0:T(8,128)}, u32[]{:S(2)}, u32[]{:S(2)}) async-start(f32[16,8,32,128]{3,2,1,0:T(8,128)} %get-tuple-element.74), calls=%async_computation.2 | async-start | bytes 4194304 | tf_op jit(solution)/shard_map/all_to_all | solution.py:384
  134.1 17.7 %shard_map.182 = (f32[2,8,8,88,128]{4,3,2,1,0:T(8,128)}, bf16[8,18,96,256]{3,2,1,0:T(8,128)(2,1)}) custom-call(f32[2]{0:T(128)S(1)} %add_convert_fusion.edge_ref, f32[8,18,88,128]{3,2,1,0:T(8,128)} %get-tuple-element.63.mid_ref, f32[8,16,88,128]{3,2,1,0:T(8,128)} %x_ref.9, f32[4,8,128]{2,1,0:T(8,128)S(1)} %copy-done.25, bf16[512,768]{1,0:T(8,128)(2,1)S(1)} %copy-done.14, ...), custom_call_target="tpu_custom_call" | custom-call | flops 1245708288 | bytes 3262529 | tf_op jit(solution)/shard_map/pallas_call | solution.py:257
  156.7 15.8 %all-to-all-done.2 = f32[16,8,32,128]{3,2,1,0:T(8,128)} async-done(((f32[16,8,32,128]{3,2,1,0:T(8,128)}), f32[16,8,32,128]{3,2,1,0:T(8,128)}, u32[]{:S(2)}, u32[]{:S(2)}) %all-to-all-start.2) | async-done | bytes 2097184 | tf_op jit(solution)/shard_map/all_to_all | solution.py:384
  197.5 13.0 %shard_map.183 = (f32[9,128,128]{2,1,0:T(8,128)S(1)}, f32[1,8,128]{2,1,0:T(8,128)S(1)}) custom-call(f32[9,128,128]{2,1,0:T(8,128)S(1)} %broadcast_in_dim.37.before_ref, bf16[8,18,96,256]{3,2,1,0:T(8,128)(2,1)} %get-tuple-element.95.act_ref, s32[2]{0:T(128)S(1)} %pad_add_fusion.refs_0_.band_ref, f32[8,8,24,128]{3,2,1,0:T(8,128)S(1)} %get-tuple-element.135.refs_1_.refs_0_, ...), custom_call_target="tpu_custom_call" | custom-call | flops 830472192 | bytes 1491457 | tf_op jit(solution)/shard_map/pallas_call | solution.py:257
  211.2 6.3 %all-to-all-start.3 = ((f32[16,8,24,128]{3,2,1,0:T(8,128)}), f32[16,8,24,128]{3,2,1,0:T(8,128)}, u32[]{:S(2)}, u32[]{:S(2)}) async-start(f32[16,8,24,128]{3,2,1,0:T(8,128)} %bitcast.114), calls=%async_computation.3 | async-start | bytes 3145728 | tf_op jit(solution)/shard_map/all_to_all | solution.py:384
  222.6 18.1 %shard_map.184 = (f32[8,16,88,128]{3,2,1,0:T(8,128)}, f32[8,16,88,128]{3,2,1,0:T(8,128)}, f32[2,8,128]{2,1,0:T(8,128)S(1)}) custom-call(s32[2]{0:T(128)S(1)} %pad_add_fusion.refs_0_.band_ref, f32[8,1,88,128]{3,2,1,0:T(8,128)S(1)} %copy-done.8, f32[8,1,88,128]{3,2,1,0:T(8,128)S(1)} %copy-done.7, f32[8,18,88,128]{3,2,1,0:T(8,128)} %get-tuple-element.63.mid_ref, ...), custom_call_target="tpu_custom_call" | custom-call | flops 1245708288 | bytes 3189761 | tf_op jit(solution)/shard_map/pallas_call | solution.py:257
  250.1 3.7 collective-permute-start.25
  253.9 4.1 %collective-permute-start.24 = (f32[8,1,88,128]{3,2,1,0:T(8,128)S(1)}, f32[8,1,88,128]{3,2,1,0:T(8,128)S(1)}, u32[]{:S(2)}, u32[]{:S(2)}) collective-permute-start(f32[8,1,88,128]{3,2,1,0:T(8,128)S(1)} %get-tuple-element.117), channel_id=1, source_target_pairs={{0,2},{2,4},{4,6},{6,8},{8,10},{10,12},{12,14},{14,16},{16,18},{18... | collective-permute-start | bytes 1081352 | tf_op jit(solution)/shard_map/ppermute | solution.py:338
  261.2 3.2 collective-permute-done.25.bot_ref
  265.1 4.4 %all-to-all-start.4 = ((f32[16,8,48,128]{3,2,1,0:T(8,128)}), f32[16,8,48,128]{3,2,1,0:T(8,128)}, u32[]{:S(2)}, u32[]{:S(2)}) async-start(f32[16,8,48,128]{3,2,1,0:T(8,128)} %bitcast.112), calls=%async_computation.4 | async-start | bytes 6291456 | tf_op jit(solution)/shard_map/all_to_all | solution.py:384
  274.2 10.4 %shard_map.187 = (f32[9,128,128]{2,1,0:T(8,128)S(1)}, f32[1,8,128]{2,1,0:T(8,128)S(1)}) custom-call(f32[9,128,128]{2,1,0:T(8,128)S(1)} %copy-done.20, bf16[8,18,96,256]{3,2,1,0:T(8,128)(2,1)} %get-tuple-element.95.act_ref, s32[2]{0:T(128)S(1)} %pad_add_fusion.refs_0_.band_ref, f32[8,8,32,128]{3,2,1,0:T(8,128)S(1)} %get-tuple-element.127.refs_2_.refs_1_, ...), custom_call_target="tpu_custom_call" | custom-call | flops 622854144 | bytes 1294849 | tf_op jit(solution)/shard_map/pallas_call | solution.py:257
  284.7 19.7 %shard_map.186 = (f32[8,16,88,128]{3,2,1,0:T(8,128)}, f32[8,16,88,128]{3,2,1,0:T(8,128)}, f32[3,8,128]{2,1,0:T(8,128)S(1)}) custom-call(f32[2]{0:T(128)S(1)} %add_convert_fusion.edge_ref, f32[8,16,88,128]{3,2,1,0:T(8,128)} %get-tuple-element.86.pre_ref, f32[8,1,88,128]{3,2,1,0:T(8,128)S(1)} %copy-done.24, ...), custom_call_target="tpu_custom_call" | custom-call | flops 1245708288 | bytes 4634625 | tf_op jit(solution)/shard_map/pallas_call | solution.py:257
  306.7 18.8 %shard_map.188 = (f32[9,128,128]{2,1,0:T(8,128)S(1)}, f32[1,8,128]{2,1,0:T(8,128)}) custom-call(f32[9,128,128]{2,1,0:T(8,128)S(1)} %broadcast_in_dim.37.before_ref, bf16[8,18,96,256]{3,2,1,0:T(8,128)(2,1)} %get-tuple-element.98.act_ref, s32[1]{0:T(128)} %constant.156.clone.1.refs_0_, f32[8,16,88,128]{3,2,1,0:T(8,128)} %get-tuple-element.99.refs_1_), custom_call_target="tpu_custom_call" | custom-call | flops 1245708288 | bytes 1753600 | tf_op jit(solution)/shard_map/pallas_call | solution.py:257
  331.3 9.9 %collective-permute-done.30 = f32[576,128]{1,0:T(8,128)S(1)} collective-permute-done((f32[576,128]{1,0:T(8,128)S(1)}, f32[576,128]{1,0:T(8,128)S(1)}, u32[]{:S(2)}, u32[]{:S(2)}) %collective-permute-start.30) | collective-permute-done | bytes 294944 | tf_op jit(solution)/shard_map/ppermute | solution.py:316
  364.5 13.6 %all-to-all-start.5 = ((f32[16,8,16,128]{3,2,1,0:T(8,128)}), f32[16,8,16,128]{3,2,1,0:T(8,128)S(1)}, u32[]{:S(2)}, u32[]{:S(2)}) async-start(f32[16,8,16,128]{3,2,1,0:T(8,128)} %bitcast.48), calls=%async_computation.5 | async-start | bytes 2097152 | tf_op jit(solution)/shard_map/all_to_all | solution.py:384
  378.5 5.6 %fusion.23 = f32[1,1,16,8,88,128]{5,4,3,2,1,0:T(8,128)} fusion(f32[88]{0:T(128)S(1)} %pad.36.clone, f32[16,8,48,128]{3,2,1,0:T(8,128)} %all-to-all-done.4, f32[16,8,24,128]{3,2,1,0:T(8,128)} %all-to-all-done.3), kind=kLoop, calls=%fused_computation.125 | loop fusion | flops 2883584 | bytes 10486112 | tf_op jit(solution)/shard_map/broadcast_in_dim | solution.py:596
  389.0 7.9 %shard_map.190 = f32[8,16,88,128]{3,2,1,0:T(8,128)} custom-call(f32[8,16,88,128]{3,2,1,0:T(8,128)S(1)} %copy-done.1, f32[8,16,88,128]{3,2,1,0:T(8,128)} %x_ref.9, f32[5,8,128]{2,1,0:T(8,128)S(1)} %copy-done.37), custom_call_target="tpu_custom_call" | custom-call | bytes 2165248 | tf_op jit(solution)/shard_map/pallas_call | solution.py:257
  398.7 4.2 %all-to-all-done.5 = f32[16,8,16,128]{3,2,1,0:T(8,128)S(1)} async-done(((f32[16,8,16,128]{3,2,1,0:T(8,128)}), f32[16,8,16,128]{3,2,1,0:T(8,128)S(1)}, u32[]{:S(2)}, u32[]{:S(2)}) %all-to-all-start.5) | async-done | bytes 1048608 | tf_op jit(solution)/shard_map/all_to_all | solution.py:384
  (255 shorter events, 149.6 us)
Async XLA Ops:
  9.1 45.5 %all-to-all-start = ((f32[16,8,24,128]{3,2,1,0:T(8,128)}), f32[16,8,24,128]{3,2,1,0:T(8,128)S(1)}, u32[]{:S(2)}, u32[]{:S(2)}) async-start(f32[16,8,24,128]{3,2,1,0:T(8,128)} %slice.164), calls=%async_computation | async-start | bytes 3145728 | tf_op jit(solution)/shard_map/all_to_all | solution.py:384
  19.6 33.3 %collective-permute-start.1 = (f32[8,2,88,128]{3,2,1,0:T(8,128)S(1)}, f32[8,2,88,128]{3,2,1,0:T(8,128)S(1)}, u32[]{:S(2)}, u32[]{:S(2)}) collective-permute-start(f32[8,2,88,128]{3,2,1,0:T(8,128)S(1)} %get-tuple-element.120), channel_id=1, source_target_pairs={{2,0},{4,2},{6,4},{8,6},{10,8},{12,10},{14,12},{16,14},{18,16},{20... | collective-permute-start | bytes 2162696 | tf_op jit(solution)/shard_map/ppermute | solution.py:338
  22.1 31.7 %collective-permute-start = (f32[8,2,88,128]{3,2,1,0:T(8,128)S(1)}, f32[8,2,88,128]{3,2,1,0:T(8,128)S(1)}, u32[]{:S(2)}, u32[]{:S(2)}) collective-permute-start(f32[8,2,88,128]{3,2,1,0:T(8,128)S(1)} %get-tuple-element.121), channel_id=1, source_target_pairs={{0,2},{2,4},{4,6},{6,8},{8,10},{10,12},{12,14},{14,16},{16,18},{18... | collective-permute-start | bytes 2162696 | tf_op jit(solution)/shard_map/ppermute | solution.py:338
  25.2 25.7 %collective-permute-start.5 = (f32[2,8,128]{2,1,0:T(8,128)S(1)}, f32[2,8,128]{2,1,0:T(8,128)S(1)}, u32[]{:S(2)}, u32[]{:S(2)}) collective-permute-start(f32[2,8,128]{2,1,0:T(8,128)S(1)} %get-tuple-element.168), channel_id=1, source_target_pairs={{0,16},{2,18},{4,20},{6,22},{8,24},{10,26},{12,28},{14,30},{16,0},... | collective-permute-start | bytes 24584 | tf_op jit(solution)/shard_map/ppermute | solution.py:316
  27.5 23.4 %collective-permute-start.4 = (f32[2,8,128]{2,1,0:T(8,128)S(1)}, f32[2,8,128]{2,1,0:T(8,128)S(1)}, u32[]{:S(2)}, u32[]{:S(2)}) collective-permute-start(f32[2,8,128]{2,1,0:T(8,128)S(1)} %get-tuple-element.168), channel_id=1, source_target_pairs={{0,8},{2,10},{4,12},{6,14},{8,0},{10,2},{12,4},{14,6},{16,24},{18,... | collective-permute-start | bytes 24584 | tf_op jit(solution)/shard_map/ppermute | solution.py:316
  27.6 24.6 %collective-permute-start.6 = (f32[2,8,128]{2,1,0:T(8,128)S(1)}, f32[2,8,128]{2,1,0:T(8,128)S(1)}, u32[]{:S(2)}, u32[]{:S(2)}) collective-permute-start(f32[2,8,128]{2,1,0:T(8,128)S(1)} %get-tuple-element.168), channel_id=1, source_target_pairs={{0,24},{2,26},{4,28},{6,30},{8,16},{10,18},{12,20},{14,22},{16,8},... | collective-permute-start | bytes 24584 | tf_op jit(solution)/shard_map/ppermute | solution.py:316
  55.8 62.0 %all-to-all-start.1 = ((f32[16,8,32,128]{3,2,1,0:T(8,128)}), f32[16,8,32,128]{3,2,1,0:T(8,128)}, u32[]{:S(2)}, u32[]{:S(2)}) async-start(f32[16,8,32,128]{3,2,1,0:T(8,128)} %get-tuple-element.67), calls=%async_computation.1 | async-start | bytes 4194304 | tf_op jit(solution)/shard_map/all_to_all | solution.py:384
  72.2 34.0 %collective-permute-start.7 = (f32[8,8,24,128]{3,2,1,0:T(8,128)}, f32[8,8,24,128]{3,2,1,0:T(8,128)S(1)}, u32[]{:S(2)}, u32[]{:S(2)}) collective-permute-start(f32[8,8,24,128]{3,2,1,0:T(8,128)} %get-tuple-element.134), channel_id=1, source_target_pairs={{0,1},{1,0},{2,3},{3,2},{4,5},{5,4},{6,7},{7,6},{8,9},{9,8},{10,11... | collective-permute-start | bytes 2359304 | tf_op jit(solution)/shard_map/ppermute | solution.py:364
  117.8 54.7 %all-to-all-start.2 = ((f32[16,8,32,128]{3,2,1,0:T(8,128)}), f32[16,8,32,128]{3,2,1,0:T(8,128)}, u32[]{:S(2)}, u32[]{:S(2)}) async-start(f32[16,8,32,128]{3,2,1,0:T(8,128)} %get-tuple-element.74), calls=%async_computation.2 | async-start | bytes 4194304 | tf_op jit(solution)/shard_map/all_to_all | solution.py:384
  129.2 24.7 %collective-permute-start.13 = (f32[8,8,32,128]{3,2,1,0:T(8,128)}, f32[8,8,32,128]{3,2,1,0:T(8,128)S(1)}, u32[]{:S(2)}, u32[]{:S(2)}) collective-permute-start(f32[8,8,32,128]{3,2,1,0:T(8,128)} %get-tuple-element.128), channel_id=1, source_target_pairs={{0,1},{1,0},{2,3},{3,2},{4,5},{5,4},{6,7},{7,6},{8,9},{9,8},{10,11... | collective-permute-start | bytes 3145736 | tf_op jit(solution)/shard_map/ppermute | solution.py:364
  155.5 25.3 %collective-permute-start.14 = (f32[8,8,24,128]{3,2,1,0:T(8,128)}, f32[8,8,24,128]{3,2,1,0:T(8,128)}, u32[]{:S(2)}, u32[]{:S(2)}) collective-permute-start(f32[8,8,24,128]{3,2,1,0:T(8,128)} %get-tuple-element.132), channel_id=1, source_target_pairs={{0,1},{1,0},{2,3},{3,2},{4,5},{5,4},{6,7},{7,6},{8,9},{9,8},{10,11... | collective-permute-start | bytes 2359304 | tf_op jit(solution)/shard_map/ppermute | solution.py:364
  178.9 11.1 %collective-permute-start.15 = (f32[8,1,88,128]{3,2,0,1:T(8,128)S(1)}, f32[8,1,88,128]{3,2,0,1:T(8,128)}, u32[]{:S(2)}, u32[]{:S(2)}) collective-permute-start(f32[8,1,88,128]{3,2,0,1:T(8,128)S(1)} %get-tuple-element.145), channel_id=1, source_target_pairs={{1,3},{3,5},{5,7},{7,9},{9,11},{11,13},{13,15},{15,17},{17,19},{19... | collective-permute-start | bytes 1081352 | tf_op jit(solution)/shard_map/ppermute | solution.py:352
  194.8 26.2 %collective-permute-start.17 = (f32[8,8,32,128]{3,2,1,0:T(8,128)}, f32[8,8,32,128]{3,2,1,0:T(8,128)}, u32[]{:S(2)}, u32[]{:S(2)}) collective-permute-start(f32[8,8,32,128]{3,2,1,0:T(8,128)} %get-tuple-element.126), channel_id=1, source_target_pairs={{0,1},{1,0},{2,3},{3,2},{4,5},{5,4},{6,7},{7,6},{8,9},{9,8},{10,11... | collective-permute-start | bytes 3145736 | tf_op jit(solution)/shard_map/ppermute | solution.py:364
  211.2 53.1 %all-to-all-start.3 = ((f32[16,8,24,128]{3,2,1,0:T(8,128)}), f32[16,8,24,128]{3,2,1,0:T(8,128)}, u32[]{:S(2)}, u32[]{:S(2)}) async-start(f32[16,8,24,128]{3,2,1,0:T(8,128)} %bitcast.114), calls=%async_computation.3 | async-start | bytes 3145728 | tf_op jit(solution)/shard_map/all_to_all | solution.py:384
  221.3 37.4 %collective-permute-start.18 = (f32[8,8,48,128]{3,2,1,0:T(8,128)S(1)}, f32[8,8,48,128]{3,2,1,0:T(8,128)S(1)}, u32[]{:S(2)}, u32[]{:S(2)}) collective-permute-start(f32[8,8,48,128]{3,2,1,0:T(8,128)S(1)} %get-tuple-element.124), channel_id=1, source_target_pairs={{0,1},{1,0},{2,3},{3,2},{4,5},{5,4},{6,7},{7,6},{8,9},{9,8},{10,11... | collective-permute-start | bytes 4718600 | tf_op jit(solution)/shard_map/ppermute | solution.py:364
  250.1 14.3 %collective-permute-start.25 = (f32[8,1,88,128]{3,2,1,0:T(8,128)S(1)}, f32[8,1,88,128]{3,2,1,0:T(8,128)S(1)}, u32[]{:S(2)}, u32[]{:S(2)}) collective-permute-start(f32[8,1,88,128]{3,2,1,0:T(8,128)S(1)} %get-tuple-element.116), channel_id=1, source_target_pairs={{2,0},{4,2},{6,4},{8,6},{10,8},{12,10},{14,12},{16,14},{18,16},{20... | collective-permute-start | bytes 1081352 | tf_op jit(solution)/shard_map/ppermute | solution.py:338
  265.1 80.2 %all-to-all-start.4 = ((f32[16,8,48,128]{3,2,1,0:T(8,128)}), f32[16,8,48,128]{3,2,1,0:T(8,128)}, u32[]{:S(2)}, u32[]{:S(2)}) async-start(f32[16,8,48,128]{3,2,1,0:T(8,128)} %bitcast.112), calls=%async_computation.4 | async-start | bytes 6291456 | tf_op jit(solution)/shard_map/all_to_all | solution.py:384
  272.0 32.4 %collective-permute-start.26 = (f32[8,8,16,128]{3,2,1,0:T(8,128)}, f32[8,8,16,128]{3,2,1,0:T(8,128)}, u32[]{:S(2)}, u32[]{:S(2)}) collective-permute-start(f32[8,8,16,128]{3,2,1,0:T(8,128)} %get-tuple-element.140), channel_id=1, source_target_pairs={{0,1},{1,0},{2,3},{3,2},{4,5},{5,4},{6,7},{7,6},{8,9},{9,8},{10,11... | collective-permute-start | bytes 1572872 | tf_op jit(solution)/shard_map/ppermute | solution.py:364
  328.4 12.8 %collective-permute-start.30 = (f32[576,128]{1,0:T(8,128)S(1)}, f32[576,128]{1,0:T(8,128)S(1)}, u32[]{:S(2)}, u32[]{:S(2)}) collective-permute-start(f32[576,128]{1,0:T(8,128)S(1)} %constant_dynamic-slice_fusion.5), channel_id=1, source_target_pairs={{0,4},{2,6},{4,0},{6,2},{8,12},{10,14},{12,8},{14,10},{16,20},{18,... | collective-permute-start | bytes 884744 | tf_op jit(solution)/shard_map/ppermute | solution.py:316
  331.2 11.2 %collective-permute-start.28 = (f32[4,8,128]{2,1,0:T(8,128)S(1)}, f32[4,8,128]{2,1,0:T(8,128)S(1)}, u32[]{:S(2)}, u32[]{:S(2)}) collective-permute-start(f32[4,8,128]{2,1,0:T(8,128)S(1)} %fusion.22), channel_id=1, source_target_pairs={{0,4},{2,6},{4,0},{6,2},{8,12},{10,14},{12,8},{14,10},{16,20},{18,... | collective-permute-start | bytes 49160 | tf_op jit(solution)/shard_map/ppermute | solution.py:316
  360.5 17.6 %collective-permute-start.39 = (f32[576,128]{1,0:T(8,128)S(1)}, f32[576,128]{1,0:T(8,128)S(1)}, u32[]{:S(2)}, u32[]{:S(2)}) collective-permute-start(f32[576,128]{1,0:T(8,128)S(1)} %broadcast_select_fusion), channel_id=1, source_target_pairs={{0,4},{2,6},{4,0},{6,2},{8,12},{10,14},{12,8},{14,10},{16,20},{18,... | collective-permute-start | bytes 884744 | tf_op jit(solution)/shard_map/ppermute | solution.py:316
  362.8 34.1 %collective-permute-start.41 = (f32[6,128]{1,0:T(8,128)S(1)}, f32[6,128]{1,0:T(8,128)S(1)}, u32[]{:S(2)}, u32[]{:S(2)}) collective-permute-start(f32[6,128]{1,0:T(8,128)S(1)} %pad_maximum_fusion.18), channel_id=1, source_target_pairs={{0,1},{1,0},{2,3},{3,2},{4,5},{5,4},{6,7},{7,6},{8,9},{9,8},{10,11... | collective-permute-start | bytes 9224 | tf_op jit(solution)/shard_map/ppermute | solution.py:316
  364.5 38.4 %all-to-all-start.5 = ((f32[16,8,16,128]{3,2,1,0:T(8,128)}), f32[16,8,16,128]{3,2,1,0:T(8,128)S(1)}, u32[]{:S(2)}, u32[]{:S(2)}) async-start(f32[16,8,16,128]{3,2,1,0:T(8,128)} %bitcast.48), calls=%async_computation.5 | async-start | bytes 2097152 | tf_op jit(solution)/shard_map/all_to_all | solution.py:384
  378.1 19.4 %collective-permute-start.40 = (f32[1152,128]{1,0:T(8,128)S(1)}, f32[1152,128]{1,0:T(8,128)S(1)}, u32[]{:S(2)}, u32[]{:S(2)}) collective-permute-start(f32[1152,128]{1,0:T(8,128)S(1)} %maximum_select_fusion.1), channel_id=1, source_target_pairs={{0,2},{2,0},{4,6},{6,4},{8,10},{10,8},{12,14},{14,12},{16,18},{18,... | collective-permute-start | bytes 1769480 | tf_op jit(solution)/shard_map/ppermute | solution.py:316
  (69 other events, 346.9 us)
